TPU v7x, 32 devices: a whole 2x2x4 slice. The times are simulated.
32 devices in a mesh: wide: 8 (over z, y), narrow: 4 (over x, core).
Axes of the slice: x: 2, y: 2, z: 4, core: 2. Of those that a mesh axis runs over, the one named last changes fastest.
Arguments:
- tokens: bfloat16 [16384, 768], P(('wide', 'narrow')), may hold values from -6 to 6
- lengths: int32 [8], P('wide'), may hold values from 1 to 2048, 12288 in all
- qkv_weight: float32 [3, 768, 768], P(None, 'wide', 'narrow'), may hold values from -0.21875 to 0.21875
- out_weight: float32 [768, 768], P('narrow', 'wide'), may hold values from -6 to 6
- gateup_weight: float32 [2, 768, 2048], P(None, 'wide', 'narrow'), may hold values from -0.21875 to 0.21875
- down_weight: float32 [2048, 768], P('narrow', 'wide'), may hold values from -0.125 to 0.125
- norm_gains: float32 [2, 768], P(None, 'wide'), may hold values from 0.5 to 1.5
- qkv_mean: float32 [3, 768, 768], P(None, 'wide', 'narrow'), may hold values from -1024 to 1024
- qkv_square: float32 [3, 768, 768], P(None, 'wide', 'narrow'), may hold values from 32768 to 147456
- out_mean: float32 [768, 768], P('narrow', 'wide'), may hold values from -32 to 32
- out_square: float32 [768, 768], P('narrow', 'wide'), may hold values from 24 to 96
- gateup_mean: float32 [2, 768, 2048], P(None, 'wide', 'narrow'), may hold values from -384 to 384
- gateup_square: float32 [2, 768, 2048], P(None, 'wide', 'narrow'), may hold values from 4096 to 16384
- down_mean: float32 [2048, 768], P('narrow', 'wide'), may hold values from -448 to 448
- down_square: float32 [2048, 768], P('narrow', 'wide'), may hold values from 5461 to 21845
- gains_mean: float32 [2, 768], P(None, 'wide'), may hold values from -1536 to 1536
- gains_square: float32 [2, 768], P(None, 'wide'), may hold values from 65536 to 262144
- cotangent: bfloat16 [16384, 768], P(('wide', 'narrow')), may hold values from -6 to 6
Outputs:
- layer_out: bfloat16 [16384, 768], P(('wide', 'narrow'))
- tokens_grad: float32 [16384, 768], P(('wide', 'narrow'))
- qkv_master: float32 [3, 768, 768], P(None, 'wide', 'narrow')
- qkv_first: float32 [3, 768, 768], P(None, 'wide', 'narrow')
- qkv_second: float32 [3, 768, 768], P(None, 'wide', 'narrow')
- out_master: float32 [768, 768], P('narrow', 'wide')
- out_first: float32 [768, 768], P('narrow', 'wide')
- out_second: float32 [768, 768], P('narrow', 'wide')
- gateup_master: float32 [2, 768, 2048], P(None, 'wide', 'narrow')
- gateup_first: float32 [2, 768, 2048], P(None, 'wide', 'narrow')
- gateup_second: float32 [2, 768, 2048], P(None, 'wide', 'narrow')
- down_master: float32 [2048, 768], P('narrow', 'wide')
- down_first: float32 [2048, 768], P('narrow', 'wide')
- down_second: float32 [2048, 768], P('narrow', 'wide')
- gains_master: float32 [2, 768], P(None, 'wide')
- gains_first: float32 [2, 768], P(None, 'wide')
- gains_second: float32 [2, 768], P(None, 'wide')
Inputs may be any that keep to these rules, and one draw needn't show every extreme that they name: `lengths`: the longest item of every draw has exactly 2048 valid patches.
All inputs are finite; a program needn't handle non-finite values. No bound on the sum of `lengths` on one device may be relied on, other than what follows from the above.
Results may differ from a plain program's by a relative error of at most 0.015.
The roundings to bfloat16 on the way count: a program that leaves them out, or rounds other values in their place, can miss the bound.
Values may be sent and summed in bfloat16 or wider, within the bound.
A program may use at most 192 MiB of HBM per device.

v0:
```python
import jax
import jax.numpy as jnp
from jax import lax
from jax.sharding import PartitionSpec as P

D = 768
HEADS = 12
HD = 64
FF = 2048
SLOT = 2048
STEP_COUNT = 5
OUT_FAN = 1


norm_eps = 1e-06
adam_eps = 1e-08
beta_first = 0.5
beta_second = 0.5
decay_rate = 0.01
gain_rate = 0.3
masked_score = -1e30


def rms_scale(rows, gain):
    return rows * lax.rsqrt(jnp.mean(rows * rows, axis=-1, keepdims=True) + norm_eps) * gain


def gelu_product(gate_part, up_part):
    return jax.nn.gelu(gate_part, approximate=True) * up_part


def adam_update(weight, mean_old, square_old, gradient, rate, decay):
    mean_new = beta_first * mean_old + (1.0 - beta_first) * gradient
    square_new = beta_second * square_old + (1.0 - beta_second) * gradient * gradient
    mean_hat = mean_new / (1.0 - beta_first**STEP_COUNT)
    square_hat = square_new / (1.0 - beta_second**STEP_COUNT)
    weight_new = weight - rate * (mean_hat / (jnp.sqrt(square_hat) + adam_eps) + decay * weight)
    return (weight_new, mean_new, square_new)


def masked_scores(query_block, key_rows, key_valid):
    scores = jnp.einsum(
        "qhd,khd->hqk", query_block, key_rows, preferred_element_type=jnp.float32
    ) * HD ** (-0.5)
    return jnp.where(key_valid[None, None, :], scores, masked_score)


def attend_forward(query_block, key_rows, value_rows, key_valid):
    scores = masked_scores(query_block, key_rows, key_valid)
    row_max = jnp.max(scores, axis=-1, keepdims=True)
    exponent = jnp.exp(scores - row_max)
    row_total = jnp.sum(exponent, axis=-1, keepdims=True)
    soft_low = (exponent / row_total).astype(jnp.bfloat16)
    attended = jnp.einsum(
        "hqk,khd->qhd", soft_low, value_rows, preferred_element_type=jnp.float32
    ).astype(jnp.bfloat16)
    return (attended, (row_max + jnp.log(row_total))[:, :, 0])


def forward_item(packed):
    query_rows, key_rows, value_rows, key_valid = packed
    slot_rows, heads_own, head_size = query_rows.shape
    block_rows = min(512, slot_rows)
    query_blocks = query_rows.reshape(slot_rows // block_rows, block_rows, heads_own, head_size)
    attended, row_lse = lax.map(
        lambda query_block: attend_forward(query_block, key_rows, value_rows, key_valid),
        query_blocks,
    )
    return (attended.reshape(slot_rows, heads_own, head_size), row_lse)


def backward_item(packed):
    query_rows, key_rows, value_rows, key_valid, grad_rows, lse_rows = packed
    slot_rows, heads_own, head_size = query_rows.shape
    block_rows = min(512, slot_rows)
    block_count = slot_rows // block_rows

    def step_block(carry, inputs):
        key_acc, value_acc = carry
        query_block, grad_block, lse_block = inputs
        scores = masked_scores(query_block, key_rows, key_valid)
        soft = jnp.exp(scores - lse_block[:, :, None])
        soft_low = soft.astype(jnp.bfloat16)
        value_acc = value_acc + jnp.einsum(
            "hqk,qhd->khd", soft_low, grad_block, preferred_element_type=jnp.float32
        )
        soft_grad = jnp.einsum(
            "qhd,khd->hqk", grad_block, value_rows, preferred_element_type=jnp.float32
        )
        row_delta = jnp.sum(soft * soft_grad, axis=-1, keepdims=True)
        score_grad = (soft * (soft_grad - row_delta)).astype(jnp.bfloat16) * HD ** (-0.5)
        query_grad = jnp.einsum(
            "hqk,khd->qhd", score_grad, key_rows, preferred_element_type=jnp.float32
        )
        key_acc = key_acc + jnp.einsum(
            "hqk,qhd->khd", score_grad, query_block, preferred_element_type=jnp.float32
        )
        return ((key_acc, value_acc), query_grad.astype(jnp.bfloat16))

    zero_acc = jnp.zeros(key_rows.shape, jnp.float32)
    query_blocks = query_rows.reshape(block_count, block_rows, heads_own, head_size)
    grad_blocks = grad_rows.reshape(block_count, block_rows, heads_own, head_size)
    (key_acc, value_acc), query_grads = lax.scan(
        step_block, (zero_acc, zero_acc), (query_blocks, grad_blocks, lse_rows)
    )
    return (
        query_grads.reshape(slot_rows, heads_own, head_size),
        key_acc.astype(jnp.bfloat16),
        value_acc.astype(jnp.bfloat16),
    )


def shards(
    tokens,
    lengths,
    qkv_weight,
    out_weight,
    gateup_weight,
    down_weight,
    norm_gains,
    qkv_mean,
    qkv_square,
    out_mean,
    out_square,
    gateup_mean,
    gateup_square,
    down_mean,
    down_square,
    gains_mean,
    gains_square,
    cotangent,
):
    rows_own = tokens.shape[0]
    narrow_count = lax.axis_size("narrow")
    rows_dev = rows_own * narrow_count
    heads_own = HEADS // narrow_count
    width_heads = heads_own * HD
    items_dev = rows_dev // SLOT
    lowered = (
        qkv_weight.astype(jnp.bfloat16),
        out_weight.astype(jnp.bfloat16),
        gateup_weight.astype(jnp.bfloat16),
        down_weight.astype(jnp.bfloat16),
        norm_gains.astype(jnp.bfloat16),
    )
    qkv_full, out_full, gateup_full, down_full, gains_full = (
        lax.all_gather(lowered[0], "wide", axis=1, tiled=True),
        lax.all_gather(lowered[1], "wide", axis=1, tiled=True),
        lax.all_gather(lowered[2], "wide", axis=1, tiled=True),
        lax.all_gather(lowered[3], "wide", axis=1, tiled=True),
        lax.all_gather(lowered[4], "wide", axis=1, tiled=True),
    )
    gain_values = gains_full.astype(jnp.float32)
    rows_full = lax.all_gather(tokens, "narrow", axis=0, tiled=True)
    rows_float = rows_full.astype(jnp.float32)
    normed_one = rms_scale(rows_float, gain_values[0]).astype(jnp.bfloat16)
    projected = jnp.einsum(
        "td,sde->ste", normed_one, qkv_full, preferred_element_type=jnp.float32
    ).astype(jnp.bfloat16)
    shaped = projected.reshape(3, items_dev, SLOT, heads_own, HD)
    valid_keys = jnp.arange(SLOT)[None, :] < lengths[:, None]
    attended, row_lse = lax.map(forward_item, (shaped[0], shaped[1], shaped[2], valid_keys))
    mixed = attended.reshape(rows_dev, width_heads)
    attn_partial = jnp.dot(mixed, out_full, preferred_element_type=jnp.float32)
    own_float = tokens.astype(jnp.float32)
    attn_own = lax.psum_scatter(attn_partial, "narrow", scatter_dimension=0, tiled=True)
    residual_own = own_float + attn_own
    residual_full = lax.all_gather(residual_own, "narrow", axis=0, tiled=True)
    normed_two = rms_scale(residual_full, gain_values[1]).astype(jnp.bfloat16)
    gateup = jnp.einsum("td,sdf->stf", normed_two, gateup_full, preferred_element_type=jnp.float32)
    hidden = gelu_product(gateup[0], gateup[1]).astype(jnp.bfloat16)
    mlp_own = lax.psum_scatter(
        jnp.dot(hidden, down_full, preferred_element_type=jnp.float32).astype(jnp.bfloat16),
        "narrow",
        scatter_dimension=0,
        tiled=True,
    ).astype(jnp.float32)
    layer_out = (residual_own + mlp_own).astype(jnp.bfloat16)
    grad_full = lax.all_gather(cotangent, "narrow", axis=0, tiled=True)
    down_grad = jnp.einsum("tf,td->fd", hidden, grad_full, preferred_element_type=jnp.float32)
    hidden_grad = jnp.einsum("td,fd->tf", grad_full, down_full, preferred_element_type=jnp.float32)
    primal_out, gelu_back = jax.vjp(gelu_product, gateup[0], gateup[1])
    gate_grad, up_grad = gelu_back(hidden_grad)
    gateup_rows = jnp.stack([gate_grad, up_grad]).astype(jnp.bfloat16)
    gateup_grad = jnp.einsum(
        "td,stf->sdf", normed_two, gateup_rows, preferred_element_type=jnp.float32
    )
    normed_two_part = jnp.einsum(
        "stf,sdf->td", gateup_rows, gateup_full, preferred_element_type=jnp.float32
    )
    normed_two_grad = lax.psum_scatter(
        normed_two_part.astype(jnp.bfloat16), "narrow", scatter_dimension=0, tiled=True
    ).astype(jnp.float32)
    primal_two, norm_two_back = jax.vjp(rms_scale, residual_own, gain_values[1])
    residual_part, gain_two_grad = norm_two_back(normed_two_grad)
    residual_grad = cotangent.astype(jnp.float32) + residual_part
    residual_low = lax.all_gather(residual_grad.astype(jnp.bfloat16), "narrow", axis=0, tiled=True)
    out_grad = jnp.einsum("te,td->ed", mixed, residual_low, preferred_element_type=jnp.float32)
    mixed_grad = jnp.einsum(
        "td,ed->te", residual_low, out_full, preferred_element_type=jnp.float32
    ).astype(jnp.bfloat16)
    grads_query, grads_key, grads_value = lax.map(
        backward_item,
        (
            shaped[0],
            shaped[1],
            shaped[2],
            valid_keys,
            mixed_grad.reshape(items_dev, SLOT, heads_own, HD),
            row_lse,
        ),
    )
    qkv_rows = jnp.stack([grads_query, grads_key, grads_value]).reshape(3, rows_dev, width_heads)
    qkv_grad = jnp.einsum("td,ste->sde", normed_one, qkv_rows, preferred_element_type=jnp.float32)
    normed_one_part = jnp.einsum(
        "ste,sde->td", qkv_rows, qkv_full, preferred_element_type=jnp.float32
    )
    normed_one_grad = lax.psum_scatter(
        normed_one_part.astype(jnp.bfloat16), "narrow", scatter_dimension=0, tiled=True
    ).astype(jnp.float32)
    primal_one, norm_one_back = jax.vjp(rms_scale, own_float, gain_values[0])
    tokens_part, gain_one_grad = norm_one_back(normed_one_grad)
    tokens_grad = residual_grad + tokens_part
    gains_grad = lax.psum(jnp.stack([gain_one_grad, gain_two_grad]), "narrow")
    reduced_qkv, reduced_out, reduced_gateup, reduced_down, reduced_gains = (
        lax.psum_scatter(qkv_grad, "wide", scatter_dimension=1, tiled=True),
        lax.psum_scatter(out_grad, "wide", scatter_dimension=1, tiled=True),
        lax.psum_scatter(gateup_grad, "wide", scatter_dimension=1, tiled=True),
        lax.psum_scatter(down_grad, "wide", scatter_dimension=1, tiled=True),
        lax.psum_scatter(gains_grad, "wide", scatter_dimension=1, tiled=True),
    )
    qkv_master, qkv_first, qkv_second = adam_update(
        qkv_weight, qkv_mean, qkv_square, reduced_qkv, D ** (-0.5), decay_rate
    )
    out_master, out_first, out_second = adam_update(
        out_weight, out_mean, out_square, reduced_out, OUT_FAN ** (-0.5), decay_rate
    )
    gateup_master, gateup_first, gateup_second = adam_update(
        gateup_weight, gateup_mean, gateup_square, reduced_gateup, D ** (-0.5), decay_rate
    )
    down_master, down_first, down_second = adam_update(
        down_weight, down_mean, down_square, reduced_down, FF ** (-0.5), decay_rate
    )
    gains_master, gains_first, gains_second = adam_update(
        norm_gains, gains_mean, gains_square, reduced_gains, gain_rate, 0.0
    )
    return (
        layer_out,
        tokens_grad,
        qkv_master,
        qkv_first,
        qkv_second,
        out_master,
        out_first,
        out_second,
        gateup_master,
        gateup_first,
        gateup_second,
        down_master,
        down_first,
        down_second,
        gains_master,
        gains_first,
        gains_second,
    )


def solution(mesh):
    return jax.shard_map(
        shards,
        mesh=mesh,
        in_specs=(
            P(("wide", "narrow"), None),
            P("wide"),
            P(None, "wide", "narrow"),
            P("narrow", "wide"),
            P(None, "wide", "narrow"),
            P("narrow", "wide"),
            P(None, "wide"),
            P(None, "wide", "narrow"),
            P(None, "wide", "narrow"),
            P("narrow", "wide"),
            P("narrow", "wide"),
            P(None, "wide", "narrow"),
            P(None, "wide", "narrow"),
            P("narrow", "wide"),
            P("narrow", "wide"),
            P(None, "wide"),
            P(None, "wide"),
            P(("wide", "narrow"), None),
        ),
        out_specs=(
            P(("wide", "narrow"), None),
            P(("wide", "narrow"), None),
            P(None, "wide", "narrow"),
            P(None, "wide", "narrow"),
            P(None, "wide", "narrow"),
            P("narrow", "wide"),
            P("narrow", "wide"),
            P("narrow", "wide"),
            P(None, "wide", "narrow"),
            P(None, "wide", "narrow"),
            P(None, "wide", "narrow"),
            P("narrow", "wide"),
            P("narrow", "wide"),
            P("narrow", "wide"),
            P(None, "wide"),
            P(None, "wide"),
            P(None, "wide"),
        ),
        check_vma=False,
    )
```

profile of v0, /device:TPU:0, one launch (start us, length us, event | category | flops | bytes accessed | tf_op | source)
XLA Modules:
  0.0 917.6 jit_solution(6565188482808327016)
XLA Ops:
  8.7 22.1 %all-gather = bf16[8,96,2]{1,2,0:T(2,128)(2,1)S(1)} all-gather(bf16[1,96,2]{1,2,0:T(2,128)(2,1)S(1)} %convert_bitcast_fusion.1), channel_id=1, replica_groups=mesh['wide'=8,'narrow'=4] {'wide'}, dimensions={0}, use_global_device_ids=true | all-gather | bytes 3456 | tf_op jit(solution)/shard_map/all_gather | solution.py:151
  33.0 35.3 %all_gather.29 = bf16[3,768,192]{2,0,1:T(4,128)(2,1)S(1)} all-gather(bf16[3,96,192]{2,0,1:T(4,128)(2,1)S(1)} %copy.106), channel_id=1, replica_groups=mesh['wide'=8,'narrow'=4] {'wide'}, dimensions={1}, use_global_device_ids=true | all-gather | bytes 995328 | tf_op jit(solution)/shard_map/all_gather | solution.py:147
  69.3 31.1 %all_gather.30 = bf16[192,768]{0,1:T(8,128)(2,1)S(1)} all-gather(bf16[192,96]{0,1:T(8,128)(2,1)S(1)} %copy.110), channel_id=1, replica_groups=mesh['wide'=8,'narrow'=4] {'wide'}, dimensions={1}, use_global_device_ids=true | all-gather | bytes 331776 | tf_op jit(solution)/shard_map/all_gather | solution.py:148
  100.3 2.6 fusion.101
  102.9 4.0 fusion.132
  108.3 39.1 %while.48 = (s32[]{:T(128)}, bf16[4,512,3,64]{1,3,2,0:T(8,128)(2,1)S(1)}, f32[4,3,512]{2,1,0:T(4,128)}, bf16[4,512,3,64]{1,3,2,0:T(8,128)(2,1)S(1)}, bf16[2048,3...) while((s32[]{:T(128)}, ...), condition=%wide.region_4.5_spmd.clone, body=%wide.region_1.4_spmd.clone.sunk | while | flops 843153920 | bytes 39778412 | solution.py:65
  111.0 2.8 fusion.202
  113.8 3.7 fusion.203
  120.7 2.8 fusion.202
  123.5 3.7 fusion.203
  130.5 2.8 fusion.202
  133.3 3.7 fusion.203
  140.3 2.8 fusion.202
  143.1 3.7 fusion.203
  149.0 3.7 fusion.154
  152.8 57.6 %reduce-scatter.15.cloned.1.call-done = f32[512,768]{1,0:T(8,128)} async-done(((f32[2048,768]{1,0:T(8,128)}), f32[512,768]{1,0:T(8,128)}) %reduce-scatter.15.cloned.1.call-update) | async-done | bytes 1572880 | tf_op jit(solution)/shard_map/reduce_scatter | solution.py:166
  210.4 3.3 multiply_reduce_fusion.2
  215.3 32.3 %all_gather.33 = bf16[512,768]{0,1:T(8,128)(2,1)S(1)} all-gather(bf16[512,96]{0,1:T(8,128)(2,1)S(1)} %convert_element_type.111), channel_id=1, replica_groups=mesh['wide'=8,'narrow'=4] {'wide'}, dimensions={1}, use_global_device_ids=true | all-gather | bytes 884736 | tf_op jit(solution)/shard_map/all_gather | solution.py:150
  247.6 12.8 %all-gather.9.cloned.1.call-done = f32[2048,768]{1,0:T(8,128)} async-done(((f32[512,768]{1,0:T(8,128)}), f32[2048,768]{1,0:T(8,128)}) %all-gather.9.cloned.1.call-update) | async-done | bytes 6291472 | tf_op jit(solution)/shard_map/all_gather | solution.py:168
  260.3 3.3 multiply_reduce_fusion.1
  263.6 43.8 %all-gather.11.cloned.1.call-done = bf16[2,768,512]{2,1,0:T(8,128)(2,1)} async-done(((bf16[2,96,512]{2,1,0:T(8,128)(2,1)}), bf16[2,768,512]{2,1,0:T(8,128)(2,1)}) %all-gather.11.cloned.1.call-update) | async-done | bytes 1572880 | tf_op jit(solution)/shard_map/all_gather | solution.py:149
  307.4 10.2 %convolution_bitcast_fusion = f32[2,2048,512]{2,1,0:T(8,128)} fusion(bf16[2,768,512]{2,1,0:T(8,128)(2,1)} %all-gather.11.cloned.1.call-done, f32[2048,768]{1,0:T(8,128)} %all-gather.9.cloned.1.call-done, f32[768]{0:T(1024)S(1)} %get-tuple-element.358, f32[2048]{0:T(1024)S(1)} %add_rsqrt_fusion), kind=kOutput, calls=%fused_computation.81 | convolution fusion | flops 3225944064 | bytes 16264192 | tf_op jit(solution)/shard_map/td,sdf->stf/dot_general | solution.py:170
  317.7 18.6 %all-gather.13.cloned.1.call-done = bf16[2048,768]{1,0:T(8,128)(2,1)} async-done(((bf16[512,768]{1,0:T(8,128)(2,1)}), bf16[2048,768]{1,0:T(8,128)(2,1)}) %all-gather.13.cloned.1.call-update) | async-done | bytes 3145744 | tf_op jit(solution)/shard_map/all_gather | solution.py:179
  336.3 8.8 fusion.116
  347.1 4.8 bitcast_convert_fusion.1
  352.0 38.1 %reduce-scatter.19.cloned.1.call-done = bf16[512,768]{1,0:T(8,128)(2,1)} async-done(((bf16[2048,768]{1,0:T(8,128)(2,1)}), bf16[512,768]{1,0:T(8,128)(2,1)}) %reduce-scatter.19.cloned.1.call-update) | async-done | bytes 786448 | tf_op jit(solution)/shard_map/reduce_scatter | solution.py:191
  390.1 2.3 fusion.122
  393.0 2.7 fusion.147
  396.2 9.4 %fusion.117 = f32[2,768,512]{1,2,0:T(8,128)} fusion(bf16[1,2048,512]{2,1,0:T(8,128)(2,1)} %copy-done.51, bf16[1,2048,512]{2,1,0:T(8,128)(2,1)} %copy-done.50, f32[2048,768]{1,0:T(8,128)} %all-gather.9.cloned.1.call-done, f32[768]{0:T(1024)S(1)} %get-tuple-element.358, f32[2048]{0:T(1024)} %copy-done.44), kind=kOutput, calls=%fused_computation.116 | convolution fusion | flops 3228041216 | bytes 13642752 | tf_op jit(solution)/shard_map/td,stf->sdf/dot_general | solution.py:185
  405.7 5.8 copy.120
  411.5 5.5 fusion.155
  417.1 7.3 all-gather.15.cloned.1.call-done
  424.5 3.1 convolution_convert_fusion.1
  431.3 4.1 convolution_bitcast_fusion.1
  436.4 234.0 %while.49 = (s32[]{:T(128)}, f32[2048,3,64]{0,2,1:T(8,128)}, f32[2048,3,64]{0,2,1:T(8,128)}, bf16[4,512,3,64]{1,3,2,0:T(8,128)(2,1)}, bf16[4,512,3,64]{1,3,2,0:T...) while((s32[]{:T(128)}, f32[2048,3,64]{0,2,1:T(8,128)}, ...), condition=%wide.region_13.14_spmd.clone, body=%wide.region_11.13_spmd.clone.sunk | while | flops 2115609600 | bytes 201588960 | solution.py:103
  439.8 5.0 fusion.219
  444.8 6.4 fusion.216
  451.2 20.8 %fusion.220 = bf16[4,512,3,64]{1,3,2,0:T(8,128)(2,1)} fusion(bf16[4,512,3,64]{1,3,2,0:T(8,128)(2,1)} %get-tuple-element.569, s32[]{:T(128)S(6)} %copy.155, bf16[2048,3,64]{0,2,1:T(8,128)(2,1)S(1)} %get-tuple-element.583, f32[3,512,2048]{2,1,0:T(8,128)} %fusion.216, f32[3,512,2048]{2,1,0:T(8,128)} %copy-done, ...), kind=kOutput, calls=%fused_computation.43.clone.1 | convolution fusion | flops 446795264 | bytes 51335172 | tf_op jit(solution)/shard_map/while/body/eval_jaxpr/while/body/eval_jaxpr/hqk,khd->qhd/dot_general | solution.py:92
  472.0 22.1 %fusion.218 = f32[2048,3,64]{0,2,1:T(8,128)} fusion(f32[3,512,2048]{2,1,0:T(8,128)} %fusion.216, f32[3,512,2048]{2,1,0:T(8,128)} %copy-done, f32[3,512]{1,0:T(4,128)S(1)} %dynamic-slice_bitcast_fusion.2, pred[2048]{0:T(1024)(128)(4,1)S(1)} %iota_compare_fusion.5, f32[2048,3,64]{0,2,1:T(8,128)} %get-tuple-element.567, pred[]{:T(512)S(6)} %compare.3, ...), kind=kOutput, calls=%fused_computation.40.clone.1 | convolution fusion | flops 447483392 | bytes 53694468 | tf_op jit(solution)/shard_map/while/body/eval_jaxpr/while/body/eval_jaxpr/hqk,qhd->khd/dot_general | solution.py:95
  497.2 5.9 fusion.219
  503.2 6.4 fusion.216
  509.5 21.5 %fusion.220 = bf16[4,512,3,64]{1,3,2,0:T(8,128)(2,1)} fusion(bf16[4,512,3,64]{1,3,2,0:T(8,128)(2,1)} %get-tuple-element.569, s32[]{:T(128)S(6)} %copy.155, bf16[2048,3,64]{0,2,1:T(8,128)(2,1)S(1)} %get-tuple-element.583, f32[3,512,2048]{2,1,0:T(8,128)} %fusion.216, f32[3,512,2048]{2,1,0:T(8,128)} %copy-done, ...), kind=kOutput, calls=%fused_computation.43.clone.1 | convolution fusion | flops 446795264 | bytes 51335172 | tf_op jit(solution)/shard_map/while/body/eval_jaxpr/while/body/eval_jaxpr/hqk,khd->qhd/dot_general | solution.py:92
  531.0 22.3 %fusion.218 = f32[2048,3,64]{0,2,1:T(8,128)} fusion(f32[3,512,2048]{2,1,0:T(8,128)} %fusion.216, f32[3,512,2048]{2,1,0:T(8,128)} %copy-done, f32[3,512]{1,0:T(4,128)S(1)} %dynamic-slice_bitcast_fusion.2, pred[2048]{0:T(1024)(128)(4,1)S(1)} %iota_compare_fusion.5, f32[2048,3,64]{0,2,1:T(8,128)} %get-tuple-element.567, pred[]{:T(512)S(6)} %compare.3, ...), kind=kOutput, calls=%fused_computation.40.clone.1 | convolution fusion | flops 447483392 | bytes 53694468 | tf_op jit(solution)/shard_map/while/body/eval_jaxpr/while/body/eval_jaxpr/hqk,qhd->khd/dot_general | solution.py:95
  556.6 5.9 fusion.219
  562.4 6.4 fusion.216
  568.8 20.8 %fusion.220 = bf16[4,512,3,64]{1,3,2,0:T(8,128)(2,1)} fusion(bf16[4,512,3,64]{1,3,2,0:T(8,128)(2,1)} %get-tuple-element.569, s32[]{:T(128)S(6)} %copy.155, bf16[2048,3,64]{0,2,1:T(8,128)(2,1)S(1)} %get-tuple-element.583, f32[3,512,2048]{2,1,0:T(8,128)} %fusion.216, f32[3,512,2048]{2,1,0:T(8,128)} %copy-done, ...), kind=kOutput, calls=%fused_computation.43.clone.1 | convolution fusion | flops 446795264 | bytes 51335172 | tf_op jit(solution)/shard_map/while/body/eval_jaxpr/while/body/eval_jaxpr/hqk,khd->qhd/dot_general | solution.py:92
  589.5 22.3 %fusion.218 = f32[2048,3,64]{0,2,1:T(8,128)} fusion(f32[3,512,2048]{2,1,0:T(8,128)} %fusion.216, f32[3,512,2048]{2,1,0:T(8,128)} %copy-done, f32[3,512]{1,0:T(4,128)S(1)} %dynamic-slice_bitcast_fusion.2, pred[2048]{0:T(1024)(128)(4,1)S(1)} %iota_compare_fusion.5, f32[2048,3,64]{0,2,1:T(8,128)} %get-tuple-element.567, pred[]{:T(512)S(6)} %compare.3, ...), kind=kOutput, calls=%fused_computation.40.clone.1 | convolution fusion | flops 447483392 | bytes 53694468 | tf_op jit(solution)/shard_map/while/body/eval_jaxpr/while/body/eval_jaxpr/hqk,qhd->khd/dot_general | solution.py:95
  615.1 5.9 fusion.219
  621.0 6.4 fusion.216
  627.3 20.5 %fusion.220 = bf16[4,512,3,64]{1,3,2,0:T(8,128)(2,1)} fusion(bf16[4,512,3,64]{1,3,2,0:T(8,128)(2,1)} %get-tuple-element.569, s32[]{:T(128)S(6)} %copy.155, bf16[2048,3,64]{0,2,1:T(8,128)(2,1)S(1)} %get-tuple-element.583, f32[3,512,2048]{2,1,0:T(8,128)} %fusion.216, f32[3,512,2048]{2,1,0:T(8,128)} %copy-done, ...), kind=kOutput, calls=%fused_computation.43.clone.1 | convolution fusion | flops 446795264 | bytes 51335172 | tf_op jit(solution)/shard_map/while/body/eval_jaxpr/while/body/eval_jaxpr/hqk,khd->qhd/dot_general | solution.py:92
  647.9 22.3 %fusion.218 = f32[2048,3,64]{0,2,1:T(8,128)} fusion(f32[3,512,2048]{2,1,0:T(8,128)} %fusion.216, f32[3,512,2048]{2,1,0:T(8,128)} %copy-done, f32[3,512]{1,0:T(4,128)S(1)} %dynamic-slice_bitcast_fusion.2, pred[2048]{0:T(1024)(128)(4,1)S(1)} %iota_compare_fusion.5, f32[2048,3,64]{0,2,1:T(8,128)} %get-tuple-element.567, pred[]{:T(512)S(6)} %compare.3, ...), kind=kOutput, calls=%fused_computation.40.clone.1 | convolution fusion | flops 447483392 | bytes 53694468 | tf_op jit(solution)/shard_map/while/body/eval_jaxpr/while/body/eval_jaxpr/hqk,qhd->khd/dot_general | solution.py:95
  670.4 2.8 copy.113
  673.2 2.8 stack.32
  680.3 3.4 fusion.128
  683.7 3.0 copy.127
  686.7 2.9 reshape.186
  689.6 6.3 bitcast_convert_fusion
  696.0 5.2 convolution_convert_fusion
  712.8 46.2 %reduce-scatter.25.cloned.1.call-done = f32[96,576]{1,0:T(8,128)} async-done(((f32[768,576]{1,0:T(8,128)}), f32[96,576]{1,0:T(8,128)}) %reduce-scatter.25.cloned.1.call-update) | async-done | bytes 221200
  767.9 30.4 %reduce-scatter.21.cloned.1.call-done = bf16[512,768]{1,0:T(8,128)(2,1)} async-done(((bf16[2048,768]{1,0:T(8,128)(2,1)}), bf16[512,768]{1,0:T(8,128)(2,1)}) %reduce-scatter.21.cloned.1.call-update) | async-done | bytes 786448 | tf_op jit(solution)/shard_map/reduce_scatter | solution.py:218
  801.2 37.7 %reduce-scatter.17.cloned.1.call-done = bf16[512,768]{1,0:T(8,128)(2,1)} async-done(((bf16[2048,768]{1,0:T(8,128)(2,1)}), bf16[512,768]{1,0:T(8,128)(2,1)}) %reduce-scatter.17.cloned.1.call-update) | async-done | bytes 786448 | tf_op jit(solution)/shard_map/reduce_scatter | solution.py:172
  838.9 3.9 fusion.125
  842.9 60.6 %reduce-scatter.29.cloned.1.call-done = f32[96,2]{1,0:T(8,128)} async-done(((f32[768,2]{1,0:T(8,128)}), f32[96,2]{1,0:T(8,128)}) %reduce-scatter.29.cloned.1.call-update) | async-done | bytes 784
  904.4 5.6 psum.8
  (225 shorter events, 71.3 us)
Async XLA Ops:
  7.2 93.1 %all-gather.7.cloned.1.call-start = ((), (), s32[]{:S(2)}) async-start(), calls=%async_computation.8 | async-start | bytes 3932160 | tf_op jit(solution)/shard_map/all_gather | solution.py:154
  7.9 202.5 %reduce-scatter.15.cloned.1.call-start = ((), (), s32[]{:S(2)}) async-start(), calls=%async_computation.9 | async-start | bytes 7864320 | tf_op jit(solution)/shard_map/reduce_scatter | solution.py:166
  69.2 37.7 %copy-start.15 = (bf16[3,768,192]{1,2,0:T(8,128)(2,1)}, bf16[3,768,192]{1,2,0:T(8,128)(2,1)S(1)}, u32[]{:S(2)}) copy-start(bf16[3,768,192]{1,2,0:T(8,128)(2,1)S(1)} %copy.107) | copy-start | bytes 2654212
  69.2 37.7 %copy-start.34 = (f32[768]{0:T(1024)}, f32[768]{0:T(1024)S(1)}, u32[]{:S(2)}) copy-start(f32[768]{0:T(1024)S(1)} %get-tuple-element.359) | copy-start | bytes 9220
  69.2 327.0 %copy-start.32 = (f32[768]{0:T(1024)}, f32[768]{0:T(1024)S(1)}, u32[]{:S(2)}) copy-start(f32[768]{0:T(1024)S(1)} %get-tuple-element.358) | copy-start | bytes 9220
  102.9 4.0 copy-start.42
  152.7 57.7 %copy-start.3 = (bf16[512,768]{1,0:T(8,128)(2,1)S(1)}, bf16[512,768]{1,0:T(8,128)(2,1)}, u32[]{:S(2)}) copy-start(bf16[512,768]{1,0:T(8,128)(2,1)} %param.22) | copy-start | bytes 2359300
  152.8 61.1 %copy-start.12 = (f32[2,96,512]{2,1,0:T(8,128)S(1)}, f32[2,96,512]{2,1,0:T(8,128)}, u32[]{:S(2)}) copy-start(f32[2,96,512]{2,1,0:T(8,128)} %param.26) | copy-start | bytes 1179652
  152.8 62.5 %copy-start.21 = (f32[512,96]{0,1:T(8,128)S(1)}, f32[512,96]{0,1:T(8,128)}, u32[]{:S(2)}) copy-start(f32[512,96]{0,1:T(8,128)} %param.27) | copy-start | bytes 589828
  152.8 107.5 %all-gather.9.cloned.1.call-start = ((), (), s32[]{:S(2)}) async-start(), calls=%async_computation.10 | async-start | bytes 7864320 | tf_op jit(solution)/shard_map/all_gather | solution.py:168
  213.8 93.6 %all-gather.11.cloned.1.call-start = ((), (), s32[]{:S(2)}) async-start(), calls=%async_computation.11 | async-start | bytes 1769472 | tf_op jit(solution)/shard_map/all_gather | solution.py:149
  214.6 121.7 %all-gather.13.cloned.1.call-start = ((), (), s32[]{:S(2)}) async-start(), calls=%async_computation.13 | async-start | bytes 3932160 | tf_op jit(solution)/shard_map/all_gather | solution.py:179
  215.2 174.9 %reduce-scatter.19.cloned.1.call-start = ((), (), s32[]{:S(2)}) async-start(), calls=%async_computation.14 | async-start | bytes 3932160 | tf_op jit(solution)/shard_map/reduce_scatter | solution.py:191
  247.5 88.7 %copy-start.16 = (bf16[512,768]{0,1:T(8,128)(2,1)}, bf16[512,768]{0,1:T(8,128)(2,1)S(1)}, u32[]{:S(2)}) copy-start(bf16[512,768]{0,1:T(8,128)(2,1)S(1)} %all_gather.33) | copy-start | bytes 2359300
  263.6 54.0 %copy-start.44 = (f32[2048]{0:T(1024)}, f32[2048]{0:T(1024)S(1)}, u32[]{:S(2)}) copy-start(f32[2048]{0:T(1024)S(1)} %add_rsqrt_fusion) | copy-start | bytes 24580
  336.3 10.8 %copy-start.48 = (bf16[2,768,512]{2,1,0:T(8,128)(2,1)S(1)}, bf16[2,768,512]{2,1,0:T(8,128)(2,1)}, u32[]{:S(2)}) copy-start(bf16[2,768,512]{2,1,0:T(8,128)(2,1)} %all-gather.11.cloned.1.call-done) | copy-start | bytes 4718596
  345.1 2.0 copy-start.51
  351.9 38.2 %copy-start.1 = (f32[512,768]{1,0:T(8,128)S(1)}, f32[512,768]{1,0:T(8,128)}, u32[]{:S(2)}) copy-start(f32[512,768]{1,0:T(8,128)} %get-tuple-element.410) | copy-start | bytes 4718596
  352.0 72.5 %all-gather.15.cloned.1.call-start = ((), (), s32[]{:S(2)}) async-start(), calls=%async_computation.15 | async-start | bytes 3932160 | tf_op jit(solution)/shard_map/all_gather | solution.py:197
  352.0 53.6 %copy-start.36 = (f32[512]{0:T(512)}, f32[512]{0:T(512)S(1)}, u32[]{:S(2)}) copy-start(f32[512]{0:T(512)S(1)} %fusion.140) | copy-start | bytes 6148
  395.8 310.3 %all-reduce.3.cloned.1.call-start = ((), (), s32[]{:S(2)}) async-start(), calls=%async_computation.21 | async-start | bytes 6291456
  411.5 295.6 %reduce-scatter.23.cloned.1.call-start = ((), (), s32[]{:S(2)}) async-start(), calls=%async_computation.17 | async-start | bytes 1769472 | tf_op jit(solution)/shard_map/reduce_scatter | solution.py:229
  417.0 14.2 %copy-start.9 = (bf16[24,8,4,512]{3,1,2,0:T(8,128)(2,1)S(1)}, bf16[24,8,4,512]{3,1,2,0:T(8,128)(2,1)}, u32[]{:S(2)}) copy-start(bf16[24,8,4,512]{3,1,2,0:T(8,128)(2,1)} %copy-done.8) | copy-start | bytes 2359300
  417.1 293.8 %reduce-scatter.27.cloned.1.call-start = ((), (), s32[]{:S(2)}) async-start(), calls=%async_computation.19 | async-start | bytes 884736
  429.0 7.4 copy-start.6
  435.4 323.6 %reduce-scatter.25.cloned.1.call-start = ((), (), s32[]{:S(2)}) async-start(), calls=%async_computation.18 | async-start | bytes 2211840
  437.9 1.8 copy-start.10
  439.7 5.0 copy-start
  497.2 5.9 copy-start
  554.7 1.8 copy-start.10
  556.5 5.9 copy-start
  615.1 5.9 copy-start
  670.4 9.9 %copy-start.11 = (bf16[2048,768]{1,0:T(8,128)(2,1)S(1)}, bf16[2048,768]{1,0:T(8,128)(2,1)}, u32[]{:S(2)}) copy-start(bf16[2048,768]{1,0:T(8,128)(2,1)} %all-gather.7.cloned.1.call-done) | copy-start | bytes 9437188
  670.4 9.9 %copy-start.35 = (f32[768]{0:T(1024)S(1)}, f32[768]{0:T(1024)}, u32[]{:S(2)}) copy-start(f32[768]{0:T(1024)} %copy-done.34) | copy-start | bytes 9220
  670.4 9.9 %copy-start.43 = (f32[2048]{0:T(1024)S(1)}, f32[2048]{0:T(1024)}, u32[]{:S(2)}) copy-start(f32[2048]{0:T(1024)} %copy-done.42) | copy-start | bytes 24580
  676.0 4.3 copy-start.18
  689.6 6.4 copy-start.17
  689.6 108.7 %reduce-scatter.21.cloned.1.call-start = ((), (), s32[]{:S(2)}) async-start(), calls=%async_computation.16 | async-start | bytes 3932160 | tf_op jit(solution)/shard_map/reduce_scatter | solution.py:218
  695.9 5.7 copy-start.14
  695.9 6.6 copy-start.26
  695.9 143.0 %reduce-scatter.17.cloned.1.call-start = ((), (), s32[]{:S(2)}) async-start(), calls=%async_computation.12 | async-start | bytes 3932160 | tf_op jit(solution)/shard_map/reduce_scatter | solution.py:172
  701.2 2.2 copy-start.27
  701.2 3.1 copy-start.49
  701.2 4.3 copy-start.38
  701.2 6.0 copy-start.22
  701.2 6.0 copy-start.28
  701.2 6.0 copy-start.29
  701.2 7.8 copy-start.13
  701.2 7.8 copy-start.24
  701.2 7.8 copy-start.25
  701.2 9.0 copy-start.40
  701.3 10.8 %copy-start.23 = (f32[192,96]{1,0:T(8,128)S(1)}, f32[192,96]{1,0:T(8,128)}, u32[]{:S(2)}) copy-start(f32[192,96]{1,0:T(8,128)} %param.25) | copy-start | bytes 221188
  701.3 10.7 %copy-start.30 = (f32[192,96]{1,0:T(8,128)S(1)}, f32[192,96]{1,0:T(8,128)}, u32[]{:S(2)}) copy-start(f32[192,96]{1,0:T(8,128)} %param.31) | copy-start | bytes 221188
  701.3 10.7 %copy-start.31 = (f32[192,96]{1,0:T(8,128)S(1)}, f32[192,96]{1,0:T(8,128)}, u32[]{:S(2)}) copy-start(f32[192,96]{1,0:T(8,128)} %param.32) | copy-start | bytes 221188
  701.3 202.2 %reduce-scatter.29.cloned.1.call-start = ((), (), s32[]{:S(2)}) async-start(), calls=%async_computation.20 | async-start | bytes 442368
  709.0 89.3 %copy-start.4 = (bf16[512,768]{1,0:T(8,128)(2,1)S(1)}, bf16[512,768]{1,0:T(8,128)(2,1)}, u32[]{:S(2)}) copy-start(bf16[512,768]{1,0:T(8,128)(2,1)} %param.22) | copy-start | bytes 2359300
  710.8 128.1 %copy-start.2 = (f32[512,768]{1,0:T(8,128)S(1)}, f32[512,768]{1,0:T(8,128)}, u32[]{:S(2)}) copy-start(f32[512,768]{1,0:T(8,128)} %get-tuple-element.410) | copy-start | bytes 4718596
  710.9 128.1 %copy-start.7 = (bf16[512,768]{1,0:T(8,128)(2,1)S(1)}, bf16[512,768]{1,0:T(8,128)(2,1)}, u32[]{:S(2)}) copy-start(bf16[512,768]{1,0:T(8,128)(2,1)} %param.39) | copy-start | bytes 2359300
  710.9 128.1 %copy-start.33 = (f32[768]{0:T(1024)S(1)}, f32[768]{0:T(1024)}, u32[]{:S(2)}) copy-start(f32[768]{0:T(1024)} %copy-done.32) | copy-start | bytes 9220
  710.9 128.1 %copy-start.37 = (f32[512]{0:T(512)S(1)}, f32[512]{0:T(512)}, u32[]{:S(2)}) copy-start(f32[512]{0:T(512)} %copy-done.36) | copy-start | bytes 6148
  761.0 39.2 %copy-start.41 = (f32[1,768]{1,0:T(1,128)S(1)}, f32[1,768]{1,0:T(1,128)}, u32[]{:S(2)}) copy-start(f32[1,768]{1,0:T(1,128)} %reshape.176) | copy-start | bytes 9220
  801.2 108.8 %copy-start.45 = (f32[2,96]{1,0:T(2,128)S(1)}, f32[2,96]{1,0:T(2,128)}, u32[]{:S(2)}) copy-start(f32[2,96]{1,0:T(2,128)} %param.28) | copy-start | bytes 2308
  801.2 108.8 %copy-start.46 = (f32[2,96]{1,0:T(2,128)S(1)}, f32[2,96]{1,0:T(2,128)}, u32[]{:S(2)}) copy-start(f32[2,96]{1,0:T(2,128)} %param.37) | copy-start | bytes 2308
  801.2 108.8 %copy-start.47 = (f32[2,96]{1,0:T(2,128)S(1)}, f32[2,96]{1,0:T(2,128)}, u32[]{:S(2)}) copy-start(f32[2,96]{1,0:T(2,128)} %param.38) | copy-start | bytes 2308
  (8 other events, 10.1 us)
Sparse Core Ops, SparseCore 0:
  9.6 31.2 all-gather.6
  152.9 57.5 reduce-scatter.14
  213.9 46.3 all-gather.8
  263.2 44.1 all-gather.10
  308.9 27.3 all-gather.12
  352.1 37.9 reduce-scatter.18
  395.9 28.5 all-gather.14
  428.0 128.9 all-reduce.2
  560.9 63.7 reduce-scatter.22
  627.8 61.3 reduce-scatter.26
  693.1 65.7 reduce-scatter.24
  761.4 36.8 reduce-scatter.20
  800.9 37.9 reduce-scatter.16
  842.0 61.3 reduce-scatter.28
where the time goes:
time: 927 us; the launch traced here: 918 us
  waiting for transfers between devices  355 us (38%)
  matrix products  319 us (34%)
  blocking collectives  126 us (14%)
  other arithmetic  52.5 us (6%)
  local copies, waits for them, and re-layouts  47.4 us (5%)
  between operations  15.7 us (2%)
    unnamed x18, waiting for transfers between devices  108 us
    dot_general x4, matrix products, step_block(): jnp.einsum('hqk,qhd->khd', score_grad, query_block, preferred_element_typ...  89 us
    dot_general x4, matrix products, step_block(): jnp.einsum('hqk,khd->qhd', score_grad, key_rows, preferred_element_type=j...  83.6 us
    reduce_scatter x1, waiting for transfers between devices, shards(): lax.psum_scatter(attn_partial, 'narrow', scatter_dimension=0, tiled=True)  57.6 us
    all_gather x1, waiting for transfers between devices, shards(): lax.all_gather(lowered[2], 'wide', axis=1, tiled=True)  43.8 us
    reduce_scatter x1, waiting for transfers between devices, shards(): lax.psum_scatter(normed_two_part.astype(jnp.bfloat16), 'narrow', scatter_...  38.1 us
    reduce_scatter x1, waiting for transfers between devices, shards(): lax.psum_scatter(jnp.dot(hidden, down_full, preferred_element_type=jnp.fl...  37.7 us
    all_gather x1, blocking collectives, shards(): lax.all_gather(lowered[0], 'wide', axis=1, tiled=True)  35.3 us
  transfers between devices with their start and end apart: 14, of which 10 were waited for; matrix products, arithmetic and copies ran while one was open for 37% of the time, Pallas kernels for 0%

commit v1 on v0

--- a/solution.py
+++ b/solution.py
@@ -1,6 +1,8 @@
 import jax
 import jax.numpy as jnp
 from jax import lax
+from jax.experimental import pallas as pl
+from jax.experimental.pallas import tpu as pltpu
 from jax.sharding import PartitionSpec as P
 
 D = 768
@@ -38,76 +40,193 @@
     return (weight_new, mean_new, square_new)
 
 
-def masked_scores(query_block, key_rows, key_valid):
-    scores = jnp.einsum(
-        "qhd,khd->hqk", query_block, key_rows, preferred_element_type=jnp.float32
-    ) * HD ** (-0.5)
-    return jnp.where(key_valid[None, None, :], scores, masked_score)
-
-
-def attend_forward(query_block, key_rows, value_rows, key_valid):
-    scores = masked_scores(query_block, key_rows, key_valid)
-    row_max = jnp.max(scores, axis=-1, keepdims=True)
-    exponent = jnp.exp(scores - row_max)
-    row_total = jnp.sum(exponent, axis=-1, keepdims=True)
-    soft_low = (exponent / row_total).astype(jnp.bfloat16)
-    attended = jnp.einsum(
-        "hqk,khd->qhd", soft_low, value_rows, preferred_element_type=jnp.float32
-    ).astype(jnp.bfloat16)
-    return (attended, (row_max + jnp.log(row_total))[:, :, 0])
-
-
-def forward_item(packed):
-    query_rows, key_rows, value_rows, key_valid = packed
-    slot_rows, heads_own, head_size = query_rows.shape
-    block_rows = min(512, slot_rows)
-    query_blocks = query_rows.reshape(slot_rows // block_rows, block_rows, heads_own, head_size)
-    attended, row_lse = lax.map(
-        lambda query_block: attend_forward(query_block, key_rows, value_rows, key_valid),
-        query_blocks,
-    )
-    return (attended.reshape(slot_rows, heads_own, head_size), row_lse)
-
-
-def backward_item(packed):
-    query_rows, key_rows, value_rows, key_valid, grad_rows, lse_rows = packed
-    slot_rows, heads_own, head_size = query_rows.shape
-    block_rows = min(512, slot_rows)
-    block_count = slot_rows // block_rows
-
-    def step_block(carry, inputs):
-        key_acc, value_acc = carry
-        query_block, grad_block, lse_block = inputs
-        scores = masked_scores(query_block, key_rows, key_valid)
-        soft = jnp.exp(scores - lse_block[:, :, None])
-        soft_low = soft.astype(jnp.bfloat16)
-        value_acc = value_acc + jnp.einsum(
-            "hqk,qhd->khd", soft_low, grad_block, preferred_element_type=jnp.float32
-        )
-        soft_grad = jnp.einsum(
-            "qhd,khd->hqk", grad_block, value_rows, preferred_element_type=jnp.float32
-        )
-        row_delta = jnp.sum(soft * soft_grad, axis=-1, keepdims=True)
-        score_grad = (soft * (soft_grad - row_delta)).astype(jnp.bfloat16) * HD ** (-0.5)
-        query_grad = jnp.einsum(
-            "hqk,khd->qhd", score_grad, key_rows, preferred_element_type=jnp.float32
-        )
-        key_acc = key_acc + jnp.einsum(
-            "hqk,qhd->khd", score_grad, query_block, preferred_element_type=jnp.float32
-        )
-        return ((key_acc, value_acc), query_grad.astype(jnp.bfloat16))
-
-    zero_acc = jnp.zeros(key_rows.shape, jnp.float32)
-    query_blocks = query_rows.reshape(block_count, block_rows, heads_own, head_size)
-    grad_blocks = grad_rows.reshape(block_count, block_rows, heads_own, head_size)
-    (key_acc, value_acc), query_grads = lax.scan(
-        step_block, (zero_acc, zero_acc), (query_blocks, grad_blocks, lse_rows)
-    )
-    return (
-        query_grads.reshape(slot_rows, heads_own, head_size),
-        key_acc.astype(jnp.bfloat16),
-        value_acc.astype(jnp.bfloat16),
-    )
+LOG2E = 1.4426950408889634
+NN = (((1,), (0,)), ((), ()))
+NT = (((1,), (1,)), ((), ()))
+QUERY_ROWS = 512
+KEY_ROWS = 512
+
+
+def pieces(value):
+    high = value.astype(jnp.bfloat16)
+    rest = value - high.astype(jnp.float32)
+    mid = rest.astype(jnp.bfloat16)
+    low = (rest - mid.astype(jnp.float32)).astype(jnp.bfloat16)
+    return high, mid, low
+
+
+def dot(left, right, dims):
+    return lax.dot_general(left, right, dims, preferred_element_type=jnp.float32)
+
+
+def key_columns(key_rows, length):
+    rows = key_rows.shape[0]
+    lane = lax.broadcasted_iota(jnp.int32, (rows, HD), 1)
+    row = lax.broadcasted_iota(jnp.int32, (rows, HD), 0)
+    mask = jnp.where(row < length, 0.0, masked_score)
+    extra = jnp.where(lane == 0, mask, jnp.where(lane < 4, 1.0, 0.0)).astype(jnp.bfloat16)
+    return jnp.concatenate([key_rows, key_rows, key_rows, extra], axis=1)
+
+
+def query_columns(query_rows, shift):
+    scaled = query_rows.astype(jnp.float32) * (LOG2E * HD ** (-0.5))
+    if shift is None:
+        lane = lax.broadcasted_iota(jnp.int32, query_rows.shape, 1)
+        extra = jnp.where(lane == 0, 1.0, 0.0).astype(jnp.bfloat16)
+    else:
+        extra = row_columns(-shift, 1.0)
+    return jnp.concatenate([*pieces(scaled), extra], axis=1)
+
+
+def row_columns(row_value, first):
+    count = row_value.shape[1]
+    high, mid, low = [piece.astype(jnp.float32) for piece in pieces(row_value)]
+    place = lax.broadcasted_iota(jnp.int32, (HD, count), 0)
+    if first is None:
+        held = jnp.where(place == 0, high, jnp.where(place == 1, mid, jnp.where(place == 2, low, 0.0)))
+    else:
+        held = jnp.where(place == 1, high, jnp.where(place == 2, mid, jnp.where(place == 3, low, 0.0)))
+        held = jnp.where(place == 0, first, held)
+    return held.T.astype(jnp.bfloat16)
+
+
+def attend_kernel(length_ref, proj_ref, out_ref, wide_ref, lse_ref, q_ref, k_ref, v_ref, s_ref):
+    slot = proj_ref.shape[1]
+    heads = proj_ref.shape[2] // HD
+    length = length_ref[0]
+    for head in range(heads):
+        span = slice(head * HD, (head + 1) * HD)
+        k_ref[head] = key_columns(proj_ref[1, :, span], length)
+        q_ref[head] = query_columns(proj_ref[0, :, span], None)
+        turned = proj_ref[2, :, span].astype(jnp.float32).T.astype(jnp.bfloat16)
+        place = lax.broadcasted_iota(jnp.int32, (16, slot), 0)
+        ones = jnp.where(place == 0, 1.0, 0.0).astype(jnp.bfloat16)
+        v_ref[head] = jnp.concatenate([turned, ones], axis=0)
+
+    @pl.loop(0, slot // QUERY_ROWS)
+    def _(block):
+        start = pl.multiple_of(block * QUERY_ROWS, QUERY_ROWS)
+        turned = []
+        for head in range(heads):
+            query = q_ref[head, pl.ds(start, QUERY_ROWS), :]
+            peak = None
+            for at in range(0, slot, KEY_ROWS):
+                score = dot(k_ref[head, pl.ds(at, KEY_ROWS), :], query, NT)
+                s_ref[pl.ds(at, KEY_ROWS), :] = score
+                most = jnp.max(score.reshape(KEY_ROWS // 8, 8, QUERY_ROWS), axis=0)
+                peak = most if peak is None else jnp.maximum(peak, most)
+            peak = jnp.max(peak, axis=0, keepdims=True)
+            total = None
+            for at in range(0, slot, KEY_ROWS):
+                soft = jnp.exp2(s_ref[pl.ds(at, KEY_ROWS), :] - peak).astype(jnp.bfloat16)
+                part = dot(v_ref[head, :, pl.ds(at, KEY_ROWS)], soft, NN)
+                total = part if total is None else total + part
+            row_sum = total[HD : HD + 1]
+            wide = total[:HD] / row_sum
+            wide_ref[head, :, pl.ds(start, QUERY_ROWS)] = wide
+            lse_ref[head, :, pl.ds(start, QUERY_ROWS)] = peak + jnp.log2(row_sum)
+            turned.append(wide)
+        joined = jnp.concatenate(turned, axis=0)
+        out_ref[pl.ds(start, QUERY_ROWS), :] = joined.T.astype(jnp.bfloat16)
+
+
+def attend_back_kernel(
+    length_ref, proj_ref, grad_ref, wide_ref, lse_ref, out_ref, q_ref, k_ref, t_ref, v_ref, dk_ref, dv_ref
+):
+    slot = proj_ref.shape[1]
+    heads = proj_ref.shape[2] // HD
+    length = length_ref[0]
+    key_turned = proj_ref[1].astype(jnp.float32).T.astype(jnp.bfloat16)
+    for head in range(heads):
+        span = slice(head * HD, (head + 1) * HD)
+        k_ref[head] = key_columns(proj_ref[1, :, span], length)
+        q_ref[head] = proj_ref[0, :, span]
+        t_ref[head] = key_turned[span]
+        lane = lax.broadcasted_iota(jnp.int32, (slot, HD), 1)
+        ones = jnp.where(lane < 3, 1.0, 0.0).astype(jnp.bfloat16)
+        v_ref[head] = jnp.concatenate([proj_ref[2, :, span], ones], axis=1)
+    dk_ref[...] = jnp.zeros_like(dk_ref)
+    dv_ref[...] = jnp.zeros_like(dv_ref)
+
+    @pl.loop(0, slot // QUERY_ROWS)
+    def _(block):
+        start = pl.multiple_of(block * QUERY_ROWS, QUERY_ROWS)
+        rows = pl.ds(start, QUERY_ROWS)
+        turned = []
+        grads = grad_ref[rows, :]
+        grads_turned = grads.astype(jnp.float32).T
+        for head in range(heads):
+            span = slice(head * HD, (head + 1) * HD)
+            query = q_ref[head, rows, :]
+            grad = grads[:, span]
+            delta = jnp.sum(grads_turned[span] * wide_ref[head, :, rows], axis=0, keepdims=True)
+            query_wide = query_columns(query, lse_ref[head, :, rows])
+            grad_wide = jnp.concatenate([grad, row_columns(-delta, None)], axis=1)
+            total = None
+            for at in range(0, slot, KEY_ROWS):
+                keys = pl.ds(at, KEY_ROWS)
+                soft = jnp.exp2(dot(k_ref[head, keys, :], query_wide, NT))
+                soft_grad = dot(v_ref[head, keys, :], grad_wide, NT)
+                soft_low = soft.astype(jnp.bfloat16)
+                score_grad = (soft * soft_grad).astype(jnp.bfloat16)
+                dv_ref[head, keys, :] += dot(soft_low, grad, NN)
+                dk_ref[head, keys, :] += dot(score_grad, query, NN)
+                part = dot(t_ref[head, :, keys], score_grad, NN)
+                total = part if total is None else total + part
+            turned.append(total * HD ** (-0.5))
+        joined = jnp.concatenate(turned, axis=0)
+        out_ref[0, rows, :] = joined.T.astype(jnp.bfloat16)
+
+    for head in range(heads):
+        span = slice(head * HD, (head + 1) * HD)
+        out_ref[1, :, span] = (dk_ref[head] * HD ** (-0.5)).astype(jnp.bfloat16)
+        out_ref[2, :, span] = dv_ref[head].astype(jnp.bfloat16)
+
+
+VMEM = pltpu.VMEM
+KERNEL_BYTES = 56 * 2**20
+
+
+def attend(lengths, proj):
+    _, slot, width = proj.shape
+    heads = width // HD
+    return pl.pallas_call(
+        attend_kernel,
+        out_shape=(
+            jax.ShapeDtypeStruct((slot, width), jnp.bfloat16),
+            jax.ShapeDtypeStruct((heads, HD, slot), jnp.float32),
+            jax.ShapeDtypeStruct((heads, 1, slot), jnp.float32),
+        ),
+        in_specs=[pl.BlockSpec(memory_space=pltpu.SMEM), pl.BlockSpec(memory_space=VMEM)],
+        out_specs=(pl.BlockSpec(memory_space=VMEM),) * 3,
+        scratch_shapes=[
+            VMEM((heads, slot, 4 * HD), jnp.bfloat16),
+            VMEM((heads, slot, 4 * HD), jnp.bfloat16),
+            VMEM((heads, HD + 16, slot), jnp.bfloat16),
+            VMEM((slot, QUERY_ROWS), jnp.float32),
+        ],
+        compiler_params=pltpu.CompilerParams(vmem_limit_bytes=KERNEL_BYTES),
+    )(lengths, proj)
+
+
+def attend_back(lengths, proj, grad, wide, lse):
+    _, slot, width = proj.shape
+    heads = width // HD
+    return pl.pallas_call(
+        attend_back_kernel,
+        out_shape=jax.ShapeDtypeStruct((3, slot, width), jnp.bfloat16),
+        in_specs=[pl.BlockSpec(memory_space=pltpu.SMEM)] + [pl.BlockSpec(memory_space=VMEM)] * 4,
+        out_specs=pl.BlockSpec(memory_space=VMEM),
+        scratch_shapes=[
+            VMEM((heads, slot, HD), jnp.bfloat16),
+            VMEM((heads, slot, 4 * HD), jnp.bfloat16),
+            VMEM((heads, HD, slot), jnp.bfloat16),
+            VMEM((heads, slot, 2 * HD), jnp.bfloat16),
+            VMEM((heads, slot, HD), jnp.float32),
+            VMEM((heads, slot, HD), jnp.float32),
+        ],
+        compiler_params=pltpu.CompilerParams(vmem_limit_bytes=KERNEL_BYTES),
+    )(lengths, proj, grad, wide, lse)
 
 
 def shards(
@@ -130,12 +249,6 @@
     gains_square,
     cotangent,
 ):
-    rows_own = tokens.shape[0]
-    narrow_count = lax.axis_size("narrow")
-    rows_dev = rows_own * narrow_count
-    heads_own = HEADS // narrow_count
-    width_heads = heads_own * HD
-    items_dev = rows_dev // SLOT
     lowered = (
         qkv_weight.astype(jnp.bfloat16),
         out_weight.astype(jnp.bfloat16),
@@ -157,10 +270,7 @@
     projected = jnp.einsum(
         "td,sde->ste", normed_one, qkv_full, preferred_element_type=jnp.float32
     ).astype(jnp.bfloat16)
-    shaped = projected.reshape(3, items_dev, SLOT, heads_own, HD)
-    valid_keys = jnp.arange(SLOT)[None, :] < lengths[:, None]
-    attended, row_lse = lax.map(forward_item, (shaped[0], shaped[1], shaped[2], valid_keys))
-    mixed = attended.reshape(rows_dev, width_heads)
+    mixed, mixed_wide, row_lse = attend(lengths, projected)
     attn_partial = jnp.dot(mixed, out_full, preferred_element_type=jnp.float32)
     own_float = tokens.astype(jnp.float32)
     attn_own = lax.psum_scatter(attn_partial, "narrow", scatter_dimension=0, tiled=True)
@@ -199,18 +309,7 @@
     mixed_grad = jnp.einsum(
         "td,ed->te", residual_low, out_full, preferred_element_type=jnp.float32
     ).astype(jnp.bfloat16)
-    grads_query, grads_key, grads_value = lax.map(
-        backward_item,
-        (
-            shaped[0],
-            shaped[1],
-            shaped[2],
-            valid_keys,
-            mixed_grad.reshape(items_dev, SLOT, heads_own, HD),
-            row_lse,
-        ),
-    )
-    qkv_rows = jnp.stack([grads_query, grads_key, grads_value]).reshape(3, rows_dev, width_heads)
+    qkv_rows = attend_back(lengths, projected, mixed_grad, mixed_wide, row_lse)
     qkv_grad = jnp.einsum("td,ste->sde", normed_one, qkv_rows, preferred_element_type=jnp.float32)
     normed_one_part = jnp.einsum(
         "ste,sde->td", qkv_rows, qkv_full, preferred_element_type=jnp.float32

time: 927 us -> 916 us (0.988)
  matrix products: 319 us -> 72.7 us
  waiting for transfers between devices: 355 us -> 543 us
  Pallas kernels: 0 us -> 67.7 us
  other arithmetic: 52.5 us -> 34.8 us
    dot_general x28 -> x0, matrix products: 251 us -> none  [the longest x4 89 us: step_block(): jnp.einsum('hqk,qhd->khd', score_grad, query_block, preferred_element_typ...]
    unnamed x18, waiting for transfers between devices: 108 us -> 233 us
    pallas_call x0 -> x2, Pallas kernels: none -> 67.7 us  [the longest x1 41.9 us: attend_back(): pl.pallas_call(attend_back_kernel, out_shape=jax.ShapeDtypeStruct((3, slo...]
    reduce_scatter x1, waiting for transfers between devices: 0.02 us -> 65.8 us  [shards(): lax.psum_scatter(down_grad, 'wide', scatter_dimension=1, tiled=True)]
    reduce_sum x4 -> x0, other arithmetic: 11.2 us -> none  [attend_forward(): row_total = jnp.sum(exponent, axis=-1, keepdims=True)]
    unnamed x119 -> x60, local copies, waits for them, and re-layouts: 27.7 us -> 29.7 us
  transfers between devices with their start and end apart: 14 -> 14, of which waited for: 10 -> 13; matrix products, arithmetic and copies ran while one was open for 37% -> 12% of each run, Pallas kernels for 0% -> 5%
where the time goes in v1:
time: 916 us; the launch traced here: 906 us
  waiting for transfers between devices  543 us (59%)
  blocking collectives  126 us (14%)
  matrix products  72.7 us (8%)
  Pallas kernels  67.7 us (7%)
  local copies, waits for them, and re-layouts  44.2 us (5%)
  other arithmetic  34.8 us (4%)
  between operations  15.8 us (2%)
    unnamed x18, waiting for transfers between devices  233 us
    reduce_scatter x1, waiting for transfers between devices, shards(): lax.psum_scatter(down_grad, 'wide', scatter_dimension=1, tiled=True)  65.8 us
    reduce_scatter x1, waiting for transfers between devices, shards(): lax.psum_scatter(attn_partial, 'narrow', scatter_dimension=0, tiled=True)  56.8 us
    all_gather x1, waiting for transfers between devices, shards(): lax.all_gather(lowered[2], 'wide', axis=1, tiled=True)  43.8 us
    pallas_call x1, Pallas kernels, attend_back(): pl.pallas_call(attend_back_kernel, out_shape=jax.ShapeDtypeStruct((3, slo...  41.9 us
    reduce_scatter x1, waiting for transfers between devices, shards(): lax.psum_scatter(normed_two_part.astype(jnp.bfloat16), 'narrow', scatter_...  37.2 us
    reduce_scatter x1, waiting for transfers between devices, shards(): lax.psum_scatter(jnp.dot(hidden, down_full, preferred_element_type=jnp.fl...  37 us
    all_gather x1, blocking collectives, shards(): lax.all_gather(lowered[0], 'wide', axis=1, tiled=True)  35.3 us
  transfers between devices with their start and end apart: 14, of which 13 were waited for; matrix products, arithmetic and copies ran while one was open for 12% of the time, Pallas kernels for 5%

profile of v1, /device:TPU:0, one launch (start us, length us, event | category | flops | bytes accessed | tf_op | source)
XLA Modules:
  0.0 906.1 jit_solution(16057497310267750503)
XLA Ops:
  8.7 22.1 %all-gather = bf16[8,96,2]{1,2,0:T(2,128)(2,1)S(1)} all-gather(bf16[1,96,2]{1,2,0:T(2,128)(2,1)S(1)} %convert_bitcast_fusion), channel_id=1, replica_groups=mesh['wide'=8,'narrow'=4] {'wide'}, dimensions={0}, use_global_device_ids=true | all-gather | bytes 3456 | tf_op jit(solution)/shard_map/all_gather | solution.py:264
  30.9 1.0 convert_element_type.74
  32.0 35.3 %all_gather.29 = bf16[3,768,192]{2,0,1:T(4,128)(2,1)S(1)} all-gather(bf16[3,96,192]{2,0,1:T(4,128)(2,1)S(1)} %copy.104), channel_id=1, replica_groups=mesh['wide'=8,'narrow'=4] {'wide'}, dimensions={1}, use_global_device_ids=true | all-gather | bytes 995328 | tf_op jit(solution)/shard_map/all_gather | solution.py:260
  67.3 2.0 copy.105
  70.2 31.3 %all_gather.30 = bf16[192,768]{0,1:T(8,128)(2,1)S(1)} all-gather(bf16[192,96]{0,1:T(8,128)(2,1)S(1)} %copy.107), channel_id=1, replica_groups=mesh['wide'=8,'narrow'=4] {'wide'}, dimensions={1}, use_global_device_ids=true | all-gather | bytes 331776 | tf_op jit(solution)/shard_map/all_gather | solution.py:261
  101.4 2.7 fusion
  104.3 3.3 fusion.31
  107.9 2.8 copy.106
  110.7 25.8 %shard_map.305 = (bf16[2048,192]{1,0:T(8,128)(2,1)}, f32[3,64,2048]{2,1,0:T(8,128)}, f32[3,1,2048]{2,1,0:T(1,128)}) custom-call(s32[1]{0:T(128)S(6)} %copy.138.length_ref, bf16[3,2048,192]{2,1,0:T(8,128)(2,1)} %bitcast.88), custom_call_target="tpu_custom_call" | custom-call | tf_op jit(solution)/shard_map/pallas_call | solution.py:193
  136.5 4.9 fusion.50
  141.9 56.8 %reduce-scatter.15.cloned.1.call-done = f32[512,768]{1,0:T(8,128)} async-done(((f32[2048,768]{1,0:T(8,128)}), f32[512,768]{1,0:T(8,128)}) %reduce-scatter.15.cloned.1.call-update) | async-done | bytes 1572880 | tf_op jit(solution)/shard_map/reduce_scatter | solution.py:276
  198.7 3.4 multiply_reduce_fusion.1
  203.6 32.1 %all_gather.33 = bf16[512,768]{0,1:T(8,128)(2,1)S(1)} all-gather(bf16[512,96]{0,1:T(8,128)(2,1)S(1)} %convert_element_type.81), channel_id=1, replica_groups=mesh['wide'=8,'narrow'=4] {'wide'}, dimensions={1}, use_global_device_ids=true | all-gather | bytes 884736 | tf_op jit(solution)/shard_map/all_gather | solution.py:263
  235.6 13.0 %all-gather.9.cloned.1.call-done = f32[2048,768]{1,0:T(8,128)} async-done(((f32[512,768]{1,0:T(8,128)}), f32[2048,768]{1,0:T(8,128)}) %all-gather.9.cloned.1.call-update) | async-done | bytes 6291472 | tf_op jit(solution)/shard_map/all_gather | solution.py:278
  248.7 3.3 multiply_reduce_fusion
  252.0 43.8 %all-gather.11.cloned.1.call-done = bf16[2,768,512]{2,1,0:T(8,128)(2,1)} async-done(((bf16[2,96,512]{2,1,0:T(8,128)(2,1)}), bf16[2,768,512]{2,1,0:T(8,128)(2,1)}) %all-gather.11.cloned.1.call-update) | async-done | bytes 1572880 | tf_op jit(solution)/shard_map/all_gather | solution.py:262
  295.7 10.2 %convolution_bitcast_fusion = f32[2,2048,512]{2,1,0:T(8,128)} fusion(bf16[2,768,512]{2,1,0:T(8,128)(2,1)} %all-gather.11.cloned.1.call-done, f32[2048,768]{1,0:T(8,128)} %all-gather.9.cloned.1.call-done, f32[768]{0:T(1024)S(1)} %get-tuple-element.95, f32[2048]{0:T(1024)S(1)} %add_rsqrt_fusion), kind=kOutput, calls=%fused_computation.11 | convolution fusion | flops 3225944064 | bytes 16264192 | tf_op jit(solution)/shard_map/td,sdf->stf/dot_general | solution.py:280
  306.0 18.6 %all-gather.13.cloned.1.call-done = bf16[2048,768]{1,0:T(8,128)(2,1)} async-done(((bf16[512,768]{1,0:T(8,128)(2,1)}), bf16[2048,768]{1,0:T(8,128)(2,1)}) %all-gather.13.cloned.1.call-update) | async-done | bytes 3145744 | tf_op jit(solution)/shard_map/all_gather | solution.py:289
  324.6 8.8 fusion.15
  333.4 1.4 copy-done.20
  335.4 4.9 bitcast_convert_fusion.1
  341.2 37.2 %reduce-scatter.19.cloned.1.call-done = bf16[512,768]{1,0:T(8,128)(2,1)} async-done(((bf16[2048,768]{1,0:T(8,128)(2,1)}), bf16[512,768]{1,0:T(8,128)(2,1)}) %reduce-scatter.19.cloned.1.call-update) | async-done | bytes 786448 | tf_op jit(solution)/shard_map/reduce_scatter | solution.py:301
  378.5 2.3 fusion.21
  382.1 2.5 fusion.44
  384.6 9.4 %fusion.16 = f32[2,768,512]{1,2,0:T(8,128)} fusion(bf16[1,2048,512]{2,1,0:T(8,128)(2,1)} %copy-done.21, bf16[1,2048,512]{2,1,0:T(8,128)(2,1)} %copy-done.20, f32[2048,768]{1,0:T(8,128)} %all-gather.9.cloned.1.call-done, f32[768]{0:T(1024)S(1)} %get-tuple-element.95, f32[2048]{0:T(1024)} %copy-done.15), kind=kOutput, calls=%fused_computation.44 | convolution fusion | flops 3228041216 | bytes 13642752 | tf_op jit(solution)/shard_map/td,stf->sdf/dot_general | solution.py:295
  394.0 5.8 copy.117
  399.9 5.5 fusion.51
  405.5 7.8 all-gather.15.cloned.1.call-done
  413.3 4.4 convolution_bitcast_fusion.1
  418.0 4.0 convolution_convert_fusion.1
  421.9 2.4 copy.108.grad_ref
  424.3 41.9 %shard_map.306 = bf16[3,2048,192]{2,1,0:T(8,128)(2,1)} custom-call(s32[1]{0:T(128)S(6)} %copy.138.length_ref, bf16[3,2048,192]{2,1,0:T(8,128)(2,1)} %bitcast.89, bf16[2048,192]{1,0:T(8,128)(2,1)} %copy.108.grad_ref, f32[3,64,2048]{2,1,0:T(8,128)} %get-tuple-element.21.wide_ref, f32[3,1,2048]{2,1,0:T(1,128)} %get-tuple-element.22.lse_ref), custom_call_target="tpu_custom_call" | custom-call | tf_op jit(solution)/shard_map/pallas_call | solution.py:215
  466.2 5.4 fusion.27
  471.6 4.2 copy.126
  475.8 4.7 reshape.103
  480.6 6.6 bitcast_convert_fusion
  487.2 5.4 convolution_convert_fusion
  493.0 1.8 copy.115
  494.8 1.8 copy.111
  496.6 1.8 copy.113
  498.5 1.2 dynamic-slice
  500.9 44.8 %all-reduce.3.cloned.1.call-done = f32[2,768,512]{2,0,1:T(2,128)} async-done(((f32[2,768,512]{2,0,1:T(2,128)}), f32[2,768,512]{2,0,1:T(2,128)}) %all-reduce.3.cloned.1.call-update) | async-done | bytes 3145744
  545.8 1.8 constant_dynamic-slice_fusion
  547.5 65.8 %reduce-scatter.23.cloned.1.call-done = f32[512,96]{0,1:T(8,128)} async-done(((f32[512,768]{0,1:T(8,128)}), f32[512,96]{0,1:T(8,128)}) %reduce-scatter.23.cloned.1.call-update) | async-done | bytes 196624 | tf_op jit(solution)/shard_map/reduce_scatter | solution.py:328
  613.3 2.1 multiply_subtract_fusion.2
  615.5 2.5 multiply_subtract_fusion
  618.0 1.3 reshape.93
  619.2 58.7 %reduce-scatter.27.cloned.1.call-done = f32[96,192]{1,0:T(8,128)} async-done(((f32[768,192]{1,0:T(8,128)}), f32[96,192]{1,0:T(8,128)}) %reduce-scatter.27.cloned.1.call-update) | async-done | bytes 73744
  678.0 1.0 copy.129
  678.9 1.7 add_subtract_fusion
  680.7 67.0 %reduce-scatter.25.cloned.1.call-done = f32[96,576]{1,0:T(8,128)} async-done(((f32[768,576]{1,0:T(8,128)}), f32[96,576]{1,0:T(8,128)}) %reduce-scatter.25.cloned.1.call-update) | async-done | bytes 221200
  747.7 1.1 reshape.104
  748.8 0.9 copy.127
  749.7 2.2 multiply_subtract_fusion.1
  751.9 1.8 copy.120
  753.8 1.9 copy.121
  755.7 0.9 copy.122
  756.5 30.4 %reduce-scatter.21.cloned.1.call-done = bf16[512,768]{1,0:T(8,128)(2,1)} async-done(((bf16[2048,768]{1,0:T(8,128)(2,1)}), bf16[512,768]{1,0:T(8,128)(2,1)}) %reduce-scatter.21.cloned.1.call-update) | async-done | bytes 786448 | tf_op jit(solution)/shard_map/reduce_scatter | solution.py:317
  786.9 1.9 fusion.22
  789.5 0.9 copy.130
  790.6 37.0 %reduce-scatter.17.cloned.1.call-done = bf16[512,768]{1,0:T(8,128)(2,1)} async-done(((bf16[2048,768]{1,0:T(8,128)(2,1)}), bf16[512,768]{1,0:T(8,128)(2,1)}) %reduce-scatter.17.cloned.1.call-update) | async-done | bytes 786448 | tf_op jit(solution)/shard_map/reduce_scatter | solution.py:282
  827.6 3.9 fusion.24
  831.5 60.6 %reduce-scatter.29.cloned.1.call-done = f32[96,2]{1,0:T(8,128)} async-done(((f32[768,2]{1,0:T(8,128)}), f32[96,2]{1,0:T(8,128)}) %reduce-scatter.29.cloned.1.call-update) | async-done | bytes 784
  893.0 5.6 psum.8
  (91 shorter events, 10.6 us)
Async XLA Ops:
  7.2 62.8 %copy-start.9 = (f32[192,96]{1,0:T(8,128)S(1)}, f32[192,96]{1,0:T(8,128)}, u32[]{:S(2)}) copy-start(f32[192,96]{1,0:T(8,128)} %param.21) | copy-start | bytes 221188
  7.2 94.2 %all-gather.7.cloned.1.call-start = ((), (), s32[]{:S(2)}) async-start(), calls=%async_computation.8 | async-start | bytes 3932160 | tf_op jit(solution)/shard_map/all_gather | solution.py:267
  7.9 190.8 %reduce-scatter.15.cloned.1.call-start = ((), (), s32[]{:S(2)}) async-start(), calls=%async_computation.9 | async-start | bytes 7864320 | tf_op jit(solution)/shard_map/reduce_scatter | solution.py:276
  101.4 2.8 copy-start.3
  104.2 3.4 copy-start.13
  141.4 57.4 %copy-start.1 = (bf16[512,768]{1,0:T(8,128)(2,1)S(1)}, bf16[512,768]{1,0:T(8,128)(2,1)}, u32[]{:S(2)}) copy-start(bf16[512,768]{1,0:T(8,128)(2,1)} %param.18) | copy-start | bytes 2359300
  141.4 60.8 %copy-start.5 = (f32[2,96,512]{2,1,0:T(8,128)S(1)}, f32[2,96,512]{2,1,0:T(8,128)}, u32[]{:S(2)}) copy-start(f32[2,96,512]{2,1,0:T(8,128)} %param.22) | copy-start | bytes 1179652
  141.4 62.1 %copy-start.8 = (f32[512,96]{0,1:T(8,128)S(1)}, f32[512,96]{0,1:T(8,128)}, u32[]{:S(2)}) copy-start(f32[512,96]{0,1:T(8,128)} %param.23) | copy-start | bytes 589828
  141.4 107.2 %all-gather.9.cloned.1.call-start = ((), (), s32[]{:S(2)}) async-start(), calls=%async_computation.10 | async-start | bytes 7864320 | tf_op jit(solution)/shard_map/all_gather | solution.py:278
  202.1 93.6 %all-gather.11.cloned.1.call-start = ((), (), s32[]{:S(2)}) async-start(), calls=%async_computation.11 | async-start | bytes 1769472 | tf_op jit(solution)/shard_map/all_gather | solution.py:262
  202.9 121.7 %all-gather.13.cloned.1.call-start = ((), (), s32[]{:S(2)}) async-start(), calls=%async_computation.13 | async-start | bytes 3932160 | tf_op jit(solution)/shard_map/all_gather | solution.py:289
  203.5 175.0 %reduce-scatter.19.cloned.1.call-start = ((), (), s32[]{:S(2)}) async-start(), calls=%async_computation.14 | async-start | bytes 3932160 | tf_op jit(solution)/shard_map/reduce_scatter | solution.py:301
  235.6 89.0 %copy-start.7 = (bf16[512,768]{0,1:T(8,128)(2,1)}, bf16[512,768]{0,1:T(8,128)(2,1)S(1)}, u32[]{:S(2)}) copy-start(bf16[512,768]{0,1:T(8,128)(2,1)S(1)} %all_gather.33) | copy-start | bytes 2359300
  251.9 54.0 %copy-start.15 = (f32[2048]{0:T(1024)}, f32[2048]{0:T(1024)S(1)}, u32[]{:S(2)}) copy-start(f32[2048]{0:T(1024)S(1)} %add_rsqrt_fusion) | copy-start | bytes 24580
  324.6 10.8 %copy-start.19 = (bf16[2,768,512]{2,1,0:T(8,128)(2,1)S(1)}, bf16[2,768,512]{2,1,0:T(8,128)(2,1)}, u32[]{:S(2)}) copy-start(bf16[2,768,512]{2,1,0:T(8,128)(2,1)} %all-gather.11.cloned.1.call-done) | copy-start | bytes 4718596
  333.4 1.4 copy-start.20
  333.4 2.0 copy-start.21
  340.3 38.1 %copy-start = (f32[512,768]{1,0:T(8,128)S(1)}, f32[512,768]{1,0:T(8,128)}, u32[]{:S(2)}) copy-start(f32[512,768]{1,0:T(8,128)} %get-tuple-element.113) | copy-start | bytes 4718596
  340.3 41.7 %copy-start.2 = (bf16[512,768]{1,0:T(8,128)(2,1)S(1)}, bf16[512,768]{1,0:T(8,128)(2,1)}, u32[]{:S(2)}) copy-start(bf16[512,768]{1,0:T(8,128)(2,1)} %param.35) | copy-start | bytes 2359300
  340.4 72.9 %all-gather.15.cloned.1.call-start = ((), (), s32[]{:S(2)}) async-start(), calls=%async_computation.15 | async-start | bytes 3932160 | tf_op jit(solution)/shard_map/all_gather | solution.py:307
  381.5 0.6 copy-start.10
  384.6 161.2 %all-reduce.3.cloned.1.call-start = ((), (), s32[]{:S(2)}) async-start(), calls=%async_computation.21 | async-start | bytes 6291456
  399.8 213.5 %reduce-scatter.23.cloned.1.call-start = ((), (), s32[]{:S(2)}) async-start(), calls=%async_computation.17 | async-start | bytes 1769472 | tf_op jit(solution)/shard_map/reduce_scatter | solution.py:328
  405.4 272.5 %reduce-scatter.27.cloned.1.call-start = ((), (), s32[]{:S(2)}) async-start(), calls=%async_computation.19 | async-start | bytes 884736
  417.7 329.9 %reduce-scatter.25.cloned.1.call-start = ((), (), s32[]{:S(2)}) async-start(), calls=%async_computation.18 | async-start | bytes 2211840
  424.3 41.9 %copy-start.4 = (bf16[2048,768]{1,0:T(8,128)(2,1)S(1)}, bf16[2048,768]{1,0:T(8,128)(2,1)}, u32[]{:S(2)}) copy-start(bf16[2048,768]{1,0:T(8,128)(2,1)} %all-gather.7.cloned.1.call-done) | copy-start | bytes 9437188
  424.3 41.9 %copy-start.14 = (f32[2048]{0:T(1024)S(1)}, f32[2048]{0:T(1024)}, u32[]{:S(2)}) copy-start(f32[2048]{0:T(1024)} %copy-done.13) | copy-start | bytes 24580
  480.5 306.4 %reduce-scatter.21.cloned.1.call-start = ((), (), s32[]{:S(2)}) async-start(), calls=%async_computation.16 | async-start | bytes 3932160 | tf_op jit(solution)/shard_map/reduce_scatter | solution.py:317
  487.2 340.4 %reduce-scatter.17.cloned.1.call-start = ((), (), s32[]{:S(2)}) async-start(), calls=%async_computation.12 | async-start | bytes 3932160 | tf_op jit(solution)/shard_map/reduce_scatter | solution.py:282
  492.6 122.8 %copy-start.6 = (f32[2,96,512]{2,1,0:T(8,128)S(1)}, f32[2,96,512]{2,1,0:T(8,128)}, u32[]{:S(2)}) copy-start(f32[2,96,512]{2,1,0:T(8,128)} %param.22) | copy-start | bytes 1179652
  492.7 399.5 %reduce-scatter.29.cloned.1.call-start = ((), (), s32[]{:S(2)}) async-start(), calls=%async_computation.20 | async-start | bytes 442368
  749.7 77.9 %copy-start.11 = (f32[512]{0:T(512)S(1)}, f32[512]{0:T(512)}, u32[]{:S(2)}) copy-start(f32[512]{0:T(512)} %copy-done.10) | copy-start | bytes 6148
  749.7 77.9 %copy-start.12 = (f32[512]{0:T(512)S(1)}, f32[512]{0:T(512)}, u32[]{:S(2)}) copy-start(f32[512]{0:T(512)} %fusion.40) | copy-start | bytes 6148
  790.5 108.2 %copy-start.16 = (f32[2,96]{1,0:T(2,128)S(1)}, f32[2,96]{1,0:T(2,128)}, u32[]{:S(2)}) copy-start(f32[2,96]{1,0:T(2,128)} %param.24) | copy-start | bytes 2308
  790.5 108.1 %copy-start.17 = (f32[2,96]{1,0:T(2,128)S(1)}, f32[2,96]{1,0:T(2,128)}, u32[]{:S(2)}) copy-start(f32[2,96]{1,0:T(2,128)} %param.33) | copy-start | bytes 2308
  790.5 108.1 %copy-start.18 = (f32[2,96]{1,0:T(2,128)S(1)}, f32[2,96]{1,0:T(2,128)}, u32[]{:S(2)}) copy-start(f32[2,96]{1,0:T(2,128)} %param.34) | copy-start | bytes 2308
Sparse Core Ops, SparseCore 0:
  9.6 31.2 all-gather.6
  141.5 57.1 reduce-scatter.14
  202.2 46.3 all-gather.8
  251.5 44.1 all-gather.10
  297.2 27.3 all-gather.12
  340.5 37.9 reduce-scatter.18
  384.7 28.5 all-gather.14
  416.9 128.8 all-reduce.2
  549.6 63.7 reduce-scatter.22
  616.5 61.4 reduce-scatter.26
  681.8 65.7 reduce-scatter.24
  750.0 36.8 reduce-scatter.20
  789.6 37.9 reduce-scatter.16
  830.7 61.3 reduce-scatter.28
